TPU v7x, 128 devices: a whole 4x4x4 slice. The times are simulated.
128 devices in a mesh: role: 2 (over z_hi), gx: 8 (over y, z_lo), gy: 8 (over x, core).
Axes of the slice: x: 4, y: 4, z: 4 (z_hi: 2, z_lo: 2; z = z_hi * 2 + z_lo), core: 2. Of those that a mesh axis runs over, the one named last changes fastest.
Arguments:
- design: float32 [256, 256, 256], P(('gx', 'gy'), None, 'role'), may hold values from 0 to 1
- force: float32 [3, 128, 128, 256], P(None, 'gx', 'gy', 'role'), may hold values from -6 to 6
- clamped_dof_mask: int32 [3, 128, 128, 256], P(None, 'gx', 'gy', 'role'), may hold values 0 or 1
- stiffness: float32 [81, 81], replicated, may hold values from -1 to 70, as said below
Outputs:
- sensitivity: float32 [256, 256, 256], P(('gx', 'gy'), None, 'role')
- displacement: float32 [3, 128, 128, 256], P(None, 'gx', 'gy', 'role')
Inputs may be any that keep to these rules, and one draw needn't show every extreme that they name: `stiffness`: symmetric, and each diagonal entry exceeds the sum of the magnitudes of the other entries of its row.
All inputs are finite; a program needn't handle non-finite values. No bound on the sum of `clamped_dof_mask` on one device may be relied on, other than what follows from the above.
Results may differ from a plain program's by a relative error of at most 0.00013.
Values sent between devices are 32-bit elements; how exact they have to be, the bound alone decides.
A program may use at most 64 MiB of HBM per device.

v0:
```python
import jax
import jax.numpy as jnp
from jax import lax
from jax.sharding import Mesh
from jax.sharding import PartitionSpec as P

ITERS = 3
RADIUS = 2
GX_GY = ("gx_0", "gx_1", "gy_0", "gy_1")
ROLE_GX_GY = ("role", "gx_0", "gx_1", "gy_0", "gy_1")
GX = ("gx_0", "gx_1")
GY = ("gy_0", "gy_1")
sharpness = 4.0
threshold = 0.5
floor_stiff = 0.001


def with_halo(block, sides, width):
    for axis, dim in sides:
        count = lax.axis_size(axis)
        forward = [(i, i + 1) for i in range(count - 1)]
        backward = [(target, source) for source, target in forward]
        low = lax.ppermute(
            lax.slice_in_dim(block, block.shape[dim] - width, None, axis=dim), axis, forward
        )
        high = lax.ppermute(lax.slice_in_dim(block, 0, width, axis=dim), axis, backward)
        block = jnp.concatenate([low, block, high], axis=dim)
    return block


def over_axes(shard, axes):
    for axis in axes:
        shard = lax.psum(shard, axis)
    return shard


def hat_list():
    return [float(RADIUS + 1 - abs(shift_idx - RADIUS)) for shift_idx in range(2 * RADIUS + 1)]


def smooth_axis(padded, axis_num, length):
    result = None
    for offset_idx, weight in enumerate(hat_list()):
        portion = weight * lax.slice_in_dim(padded, offset_idx, offset_idx + length, axis=axis_num)
        result = portion if result is None else result + portion
    return result


def axis_count(start, length, extent):
    places = start + jnp.arange(length, dtype=jnp.int32)
    counted = jnp.zeros((length,), jnp.float32)
    for offset_idx, weight in enumerate(hat_list()):
        target = places + (offset_idx - RADIUS)
        inside = jnp.logical_and(target >= 0, target < extent)
        counted = counted + weight * inside.astype(jnp.float32)
    return counted


def slab_weight(shape):
    extent_x, extent_y, extent_z = shape
    along_x = axis_count(
        lax.axis_index(GX_GY) * extent_x, extent_x, extent_x * lax.axis_size(GX_GY)
    )
    along_y = axis_count(0, extent_y, extent_y)
    along_z = axis_count(
        lax.axis_index("role") * extent_z, extent_z, extent_z * lax.axis_size("role")
    )
    return along_x[:, None, None] * along_y[None, :, None] * along_z[None, None, :]


def slab_smooth(field):
    extent_x, extent_y, extent_z = field.shape
    padded = with_halo(field, (("role", 2), (GX_GY, 0)), RADIUS)
    padded = jnp.pad(padded, ((0, 0), (RADIUS, RADIUS), (0, 0)))
    return smooth_axis(smooth_axis(smooth_axis(padded, 2, extent_z), 1, extent_y), 0, extent_x)


def heaviside_projection(values):
    scaled = jnp.tanh(sharpness * threshold) + jnp.tanh(sharpness * (1.0 - threshold))
    return (jnp.tanh(sharpness * threshold) + jnp.tanh(sharpness * (values - threshold))) / scaled


def slope(values):
    scaled = jnp.tanh(sharpness * threshold) + jnp.tanh(sharpness * (1.0 - threshold))
    bent = jnp.tanh(sharpness * (values - threshold))
    return sharpness * (1.0 - bent * bent) / scaled


def element_mean(fine):
    count_x = fine.shape[0] // 4
    count_y = fine.shape[1] // 4
    count_z = fine.shape[2] // 2
    return fine.reshape(count_x, 4, count_y, 4, count_z, 2).mean(axis=(1, 3, 5))


def spread(elements):
    count_x, count_y, count_z = elements.shape
    widened = jnp.broadcast_to(
        elements[:, None, :, None, :, None], (count_x, 4, count_y, 4, count_z, 2)
    )
    return widened.reshape(4 * count_x, 4 * count_y, 2 * count_z)


def corner_table(node_len):
    elem_len = (node_len - 1) // 2
    nodes = jnp.arange(node_len, dtype=jnp.int32)[None, :, None]
    elems = jnp.arange(elem_len, dtype=jnp.int32)[None, None, :]
    corners = jnp.arange(3, dtype=jnp.int32)[:, None, None]
    return (nodes == 2 * elems + corners).astype(jnp.float32)


def fold_table(node_len):
    rows = jnp.arange(node_len + 2, dtype=jnp.int32)[:, None]
    cols = jnp.arange(node_len, dtype=jnp.int32)[None, :]
    target = jnp.clip(rows - 1, 0, node_len - 1)
    return (target == cols).astype(jnp.float32)


def split_axis(values, axis_num):
    half_len = (values.shape[axis_num] - 1) // 2
    pieces = [
        lax.slice_in_dim(values, corner, corner + 2 * half_len - 1, stride=2, axis=axis_num)
        for corner in range(3)
    ]
    return jnp.stack(pieces, axis=0)


def split_nodes(values):
    stacked = split_axis(values, 1)
    stacked = split_axis(stacked, 3)
    table = corner_table(values.shape[3])
    stacked = jnp.einsum(
        "baqxyk,ckg->cbaqxyg",
        stacked,
        table,
        precision=lax.Precision.HIGHEST,
        preferred_element_type=jnp.float32,
    )
    return stacked.reshape(81, -1)


def merge_axis(parts, axis_num):
    opening = parts[0]
    middle = parts[1]
    closing = parts[2]
    length = opening.shape[axis_num]
    before = [(0, 0)] * opening.ndim
    before[axis_num] = (0, 1)
    behind = [(0, 0)] * opening.ndim
    behind[axis_num] = (1, 0)
    evens = jnp.pad(opening, before) + jnp.pad(closing, behind)
    leading = lax.slice_in_dim(evens, 0, length, axis=axis_num)
    ending = lax.slice_in_dim(evens, length, length + 1, axis=axis_num)
    braided = jnp.stack([leading, middle], axis=axis_num + 1)
    new_shape = list(leading.shape)
    new_shape[axis_num] = 2 * length
    return jnp.concatenate([braided.reshape(new_shape), ending], axis=axis_num)


def merge_nodes(stiffness_product, element_shape):
    reshaped = stiffness_product.reshape((3, 3, 3, 3) + tuple(element_shape))
    table = corner_table(2 * element_shape[2] + 1)
    merged = jnp.einsum(
        "cbaqxyg,ckg->baqxyk",
        reshaped,
        table,
        precision=lax.Precision.HIGHEST,
        preferred_element_type=jnp.float32,
    )
    merged = merge_axis(merged, 3)
    return merge_axis(merged, 1)


def fold_axis(padded, axis_num):
    inner_len = padded.shape[axis_num] - 2
    below = lax.slice_in_dim(padded, 0, 1, axis=axis_num)
    above = lax.slice_in_dim(padded, inner_len + 1, inner_len + 2, axis=axis_num)
    lowest = lax.slice_in_dim(padded, 1, 2, axis=axis_num) + below
    highest = lax.slice_in_dim(padded, inner_len, inner_len + 1, axis=axis_num) + above
    centre = lax.slice_in_dim(padded, 2, inner_len, axis=axis_num)
    return jnp.concatenate([lowest, centre, highest], axis=axis_num)


def shared_sum(values):
    padded = with_halo(values, (("role", 3), (GX, 1), (GY, 2)), 1)
    folded = fold_axis(fold_axis(padded, 1), 2)
    table = fold_table(values.shape[3])
    return jnp.einsum(
        "qxyk,kn->qxyn",
        folded,
        table,
        precision=lax.Precision.HIGHEST,
        preferred_element_type=jnp.float32,
    )


def inner_sum(left, right):
    local_part = jnp.sum((left * right)[:, :-1, :-1, :-1])
    return over_axes(local_part, ROLE_GX_GY)


def conjugate_gradient_solve(operate, rhs):
    solution = jnp.zeros_like(rhs)
    residual = rhs
    direction = rhs
    current = inner_sum(residual, residual)
    for sweep in range(ITERS):
        applied = operate(direction)
        step_len = current / inner_sum(direction, applied)
        solution = solution + step_len * direction
        residual = residual - step_len * applied
        updated = inner_sum(residual, residual)
        direction = residual + updated / current * direction
        current = updated
    return solution


def on_device(design, force, clamped_dof_mask, stiffness):
    filter_weight_grid = slab_weight(design.shape)
    filtered = slab_smooth(design) / filter_weight_grid
    density_slab = element_mean(heaviside_projection(filtered))
    density = lax.all_to_all(density_slab, GY, split_axis=1, concat_axis=0, tiled=True)
    factor = floor_stiff + (1.0 - floor_stiff) * density**3
    behind = ((0, 0), (0, 1), (0, 1), (0, 1))
    owned = jnp.concatenate([force, (1 - clamped_dof_mask).astype(jnp.float32)], axis=0)
    shared = shared_sum(jnp.pad(owned, behind))
    free = shared[3:]
    rhs = free * shared[:3]
    scales = factor.reshape(-1)

    def operate(values):
        columns = split_nodes(free * values)
        stiffness_product = (
            jnp.dot(
                stiffness,
                columns,
                precision=lax.Precision.HIGHEST,
                preferred_element_type=jnp.float32,
            )
            * scales[None, :]
        )
        return free * shared_sum(merge_nodes(stiffness_product, factor.shape))

    solution = conjugate_gradient_solve(operate, rhs)
    columns = split_nodes(solution)
    energy = jnp.sum(
        columns
        * jnp.dot(
            stiffness, columns, precision=lax.Precision.HIGHEST, preferred_element_type=jnp.float32
        ),
        axis=0,
    ).reshape(factor.shape)
    element_grad = -3.0 * density**2 * (1.0 - floor_stiff) * energy / 32.0
    slab_grad = lax.all_to_all(element_grad, GY, split_axis=0, concat_axis=1, tiled=True)
    voxel_grad = spread(slab_grad) * slope(filtered)
    sensitivity = slab_smooth(voxel_grad / filter_weight_grid)
    return (sensitivity, solution[:, :-1, :-1, :-1])


def solution(mesh):
    torus = Mesh(
        mesh.devices.reshape(mesh.shape["role"], 4, 2, 4, 2),
        ("role", "gx_0", "gx_1", "gy_0", "gy_1"),
    )
    return jax.shard_map(
        on_device,
        mesh=torus,
        in_specs=(P(GX_GY, None, "role"), P(None, GX, GY, "role"), P(None, GX, GY, "role"), P()),
        out_specs=(P(GX_GY, None, "role"), P(None, GX, GY, "role")),
        check_vma=False,
    )
```

profile of v0, /device:TPU:39, one launch (start us, length us, event | category | flops | bytes accessed | tf_op | source)
XLA Modules:
  0.0 574.3 jit_solution(5358044814999670989)
XLA Ops:
  0.7 4.7 collective-permute-start.4
  17.8 9.4 %collective-permute-done.5 = f32[6,17,17,1]{2,3,1,0:T(1,128)S(1)} collective-permute-done((f32[6,17,17,1]{2,3,1,0:T(1,128)S(1)}, f32[6,17,17,1]{2,3,1,0:T(1,128)S(1)}, u32[]{:S(2)}, u32[]{:S(2)}) %collective-permute-start.5) | collective-permute-done | bytes 6968 | tf_op jit(solution)/shard_map/ppermute | solution.py:26
  42.9 5.7 collective-permute-start.9
  62.8 5.8 %slice.538 = f32[3,3,8,8,129]{4,3,2,1,0:T(8,128)} slice(f32[3,3,8,17,129]{4,3,2,1,0:T(8,128)} %pad_maximum_fusion.2), slice={[0:3:1], [0:3:1], [0:8:1], [2:17:2], [0:129:1]} | slice | bytes 594432 | tf_op jit(solution)/shard_map/slice | solution.py:122
  68.6 5.7 slice.537
  74.3 5.7 slice.536
  84.9 5.7 reduce_sum.80
  95.6 6.4 %all-to-all-start = ((f32[8,1,512]{2,1,0:T(1,128)}), f32[8,1,512]{2,1,0:T(1,128)S(1)}, u32[]{:S(2)}, u32[]{:S(2)}) async-start(f32[8,1,512]{2,1,0:T(1,128)} %reshape.284), calls=%async_computation | async-start | bytes 32768 | tf_op jit(solution)/shard_map/all_to_all | solution.py:222
  102.0 4.4 fusion.40
  152.9 5.8 %collective-permute-start.15 = (f32[3,19,1,131]{3,2,1,0:T(1,128)S(1)}, f32[3,19,1,131]{3,2,1,0:T(1,128)S(1)}, u32[]{:S(2)}, u32[]{:S(2)}) collective-permute-start(f32[3,19,1,131]{3,2,1,0:T(1,128)S(1)} %get-tuple-element.31), channel_id=1, source_target_pairs={{1,0},{2,1},{3,2},{4,3},{5,4},{6,5},{7,6},{9,8},{10,9},{11,10},{12... | collective-permute-start | bytes 89612 | tf_op jit(solution)/shard_map/ppermute | solution.py:26
  164.5 5.9 %all-reduce.19 = (f32[]{:T(128)}, f32[]{:T(128)}) all-reduce(f32[]{:T(128)} %get-tuple-element.3, f32[]{:T(128)} %get-tuple-element.2), channel_id=1, replica_groups=mesh['role'=2,'gx_0'=4,'gx_1'=2,'gy_0'=4,'gy_1'=2] {'role'}, use_global_device_ids=true, to_apply=%region_3.4 | all-reduce | flops 2 | bytes 16 | tf_op jit(solution)/shard_map/psum | solution.py:33
  170.5 7.9 %all-reduce.16 = (f32[]{:T(128)}, f32[]{:T(128)}) all-reduce(f32[]{:T(128)} %get-tuple-element.12, f32[]{:T(128)} %get-tuple-element.13), channel_id=1, replica_groups=mesh['role'=2,'gx_0'=4,'gx_1'=2,'gy_0'=4,'gy_1'=2] {'gx_0'}, use_global_device_ids=true, to_apply=%region_4.5 | all-reduce | flops 2 | bytes 16 | tf_op jit(solution)/shard_map/psum | solution.py:33
  178.4 4.4 all-reduce.18
  182.8 9.5 %all-reduce.15 = (f32[]{:T(128)}, f32[]{:T(128)}) all-reduce(f32[]{:T(128)} %get-tuple-element.10, f32[]{:T(128)} %get-tuple-element.11), channel_id=1, replica_groups=mesh['role'=2,'gx_0'=4,'gx_1'=2,'gy_0'=4,'gy_1'=2] {'gy_0'}, use_global_device_ids=true, to_apply=%region_6.7 | all-reduce | flops 2 | bytes 16 | tf_op jit(solution)/shard_map/psum | solution.py:33
  192.3 8.4 %all-reduce.17 = (f32[]{:T(128)}, f32[]{:T(128)}) all-reduce(f32[]{:T(128)} %get-tuple-element.4, f32[]{:T(128)} %get-tuple-element.5), channel_id=1, replica_groups=mesh['role'=2,'gx_0'=4,'gx_1'=2,'gy_0'=4,'gy_1'=2] {'gy_1'}, use_global_device_ids=true, to_apply=%region_7.8 | all-reduce | flops 2 | bytes 16 | tf_op jit(solution)/shard_map/psum | solution.py:33
  205.6 5.9 %psum.220 = f32[]{:T(128)} all-reduce(f32[]{:T(128)} %fusion.97), channel_id=1, replica_groups=mesh['role'=2,'gx_0'=4,'gx_1'=2,'gy_0'=4,'gy_1'=2] {'role'}, use_global_device_ids=true, to_apply=%region_15.16 | all-reduce | flops 1 | bytes 8 | tf_op jit(solution)/shard_map/psum | solution.py:33
  211.5 7.0 %psum.221 = f32[]{:T(128)} all-reduce(f32[]{:T(128)} %psum.220), channel_id=1, replica_groups=mesh['role'=2,'gx_0'=4,'gx_1'=2,'gy_0'=4,'gy_1'=2] {'gx_0'}, use_global_device_ids=true, to_apply=%region_16.17 | all-reduce | flops 1 | bytes 8 | tf_op jit(solution)/shard_map/psum | solution.py:33
  218.5 4.4 psum.222
  222.9 8.6 %psum.223 = f32[]{:T(128)} all-reduce(f32[]{:T(128)} %psum.222), channel_id=1, replica_groups=mesh['role'=2,'gx_0'=4,'gx_1'=2,'gy_0'=4,'gy_1'=2] {'gy_0'}, use_global_device_ids=true, to_apply=%region_18.19 | all-reduce | flops 1 | bytes 8 | tf_op jit(solution)/shard_map/psum | solution.py:33
  231.5 9.8 %psum.224 = f32[]{:T(128)} all-reduce(f32[]{:T(128)} %psum.223), channel_id=1, replica_groups=mesh['role'=2,'gx_0'=4,'gx_1'=2,'gy_0'=4,'gy_1'=2] {'gy_1'}, use_global_device_ids=true, to_apply=%region_19.20 | all-reduce | flops 1 | bytes 8 | tf_op jit(solution)/shard_map/psum | solution.py:33
  247.7 4.9 slice.572
  252.6 5.7 slice.571
  258.3 5.7 slice.570
  263.9 4.4 fusion.39
  295.9 4.3 collective-permute-done.17
  313.4 5.9 %collective-permute-start.21 = (f32[3,19,1,131]{3,2,1,0:T(1,128)S(1)}, f32[3,19,1,131]{3,2,1,0:T(1,128)S(1)}, u32[]{:S(2)}, u32[]{:S(2)}) collective-permute-start(f32[3,19,1,131]{3,2,1,0:T(1,128)S(1)} %get-tuple-element.29), channel_id=1, source_target_pairs={{1,0},{2,1},{3,2},{4,3},{5,4},{6,5},{7,6},{9,8},{10,9},{11,10},{12... | collective-permute-start | bytes 89612 | tf_op jit(solution)/shard_map/ppermute | solution.py:26
  325.0 6.0 %psum.225 = f32[]{:T(128)} all-reduce(f32[]{:T(128)} %fusion.96), channel_id=1, replica_groups=mesh['role'=2,'gx_0'=4,'gx_1'=2,'gy_0'=4,'gy_1'=2] {'role'}, use_global_device_ids=true, to_apply=%region_21.22 | all-reduce | flops 1 | bytes 8 | tf_op jit(solution)/shard_map/psum | solution.py:33
  331.0 6.7 %psum.226 = f32[]{:T(128)} all-reduce(f32[]{:T(128)} %psum.225), channel_id=1, replica_groups=mesh['role'=2,'gx_0'=4,'gx_1'=2,'gy_0'=4,'gy_1'=2] {'gx_0'}, use_global_device_ids=true, to_apply=%region_22.23 | all-reduce | flops 1 | bytes 8 | tf_op jit(solution)/shard_map/psum | solution.py:33
  337.7 4.8 psum.227
  342.4 10.6 %psum.228 = f32[]{:T(128)} all-reduce(f32[]{:T(128)} %psum.227), channel_id=1, replica_groups=mesh['role'=2,'gx_0'=4,'gx_1'=2,'gy_0'=4,'gy_1'=2] {'gy_0'}, use_global_device_ids=true, to_apply=%region_24.25 | all-reduce | flops 1 | bytes 8 | tf_op jit(solution)/shard_map/psum | solution.py:33
  353.0 6.8 %psum.229 = f32[]{:T(128)} all-reduce(f32[]{:T(128)} %psum.228), channel_id=1, replica_groups=mesh['role'=2,'gx_0'=4,'gx_1'=2,'gy_0'=4,'gy_1'=2] {'gy_1'}, use_global_device_ids=true, to_apply=%region_25.26 | all-reduce | flops 1 | bytes 8 | tf_op jit(solution)/shard_map/psum | solution.py:33
  364.8 6.0 %psum.230 = f32[]{:T(128)} all-reduce(f32[]{:T(128)} %fusion.95), channel_id=1, replica_groups=mesh['role'=2,'gx_0'=4,'gx_1'=2,'gy_0'=4,'gy_1'=2] {'role'}, use_global_device_ids=true, to_apply=%region_27.28 | all-reduce | flops 1 | bytes 8 | tf_op jit(solution)/shard_map/psum | solution.py:33
  370.7 8.4 %psum.231 = f32[]{:T(128)} all-reduce(f32[]{:T(128)} %psum.230), channel_id=1, replica_groups=mesh['role'=2,'gx_0'=4,'gx_1'=2,'gy_0'=4,'gy_1'=2] {'gx_0'}, use_global_device_ids=true, to_apply=%region_28.29 | all-reduce | flops 1 | bytes 8 | tf_op jit(solution)/shard_map/psum | solution.py:33
  379.1 4.5 psum.232
  383.6 8.6 %psum.233 = f32[]{:T(128)} all-reduce(f32[]{:T(128)} %psum.232), channel_id=1, replica_groups=mesh['role'=2,'gx_0'=4,'gx_1'=2,'gy_0'=4,'gy_1'=2] {'gy_0'}, use_global_device_ids=true, to_apply=%region_30.31 | all-reduce | flops 1 | bytes 8 | tf_op jit(solution)/shard_map/psum | solution.py:33
  392.2 9.5 %psum.234 = f32[]{:T(128)} all-reduce(f32[]{:T(128)} %psum.233), channel_id=1, replica_groups=mesh['role'=2,'gx_0'=4,'gx_1'=2,'gy_0'=4,'gy_1'=2] {'gy_1'}, use_global_device_ids=true, to_apply=%region_31.32 | all-reduce | flops 1 | bytes 8 | tf_op jit(solution)/shard_map/psum | solution.py:33
  450.0 5.9 %collective-permute-start.27 = (f32[3,19,1,131]{3,2,1,0:T(1,128)S(1)}, f32[3,19,1,131]{3,2,1,0:T(1,128)S(1)}, u32[]{:S(2)}, u32[]{:S(2)}) collective-permute-start(f32[3,19,1,131]{3,2,1,0:T(1,128)S(1)} %get-tuple-element.27), channel_id=1, source_target_pairs={{1,0},{2,1},{3,2},{4,3},{5,4},{6,5},{7,6},{9,8},{10,9},{11,10},{12... | collective-permute-start | bytes 89612 | tf_op jit(solution)/shard_map/ppermute | solution.py:26
  460.6 5.9 %psum.235 = f32[]{:T(128)} all-reduce(f32[]{:T(128)} %fusion.94), channel_id=1, replica_groups=mesh['role'=2,'gx_0'=4,'gx_1'=2,'gy_0'=4,'gy_1'=2] {'role'}, use_global_device_ids=true, to_apply=%region_33.34 | all-reduce | flops 1 | bytes 8 | tf_op jit(solution)/shard_map/psum | solution.py:33
  466.5 6.6 %psum.236 = f32[]{:T(128)} all-reduce(f32[]{:T(128)} %psum.235), channel_id=1, replica_groups=mesh['role'=2,'gx_0'=4,'gx_1'=2,'gy_0'=4,'gy_1'=2] {'gx_0'}, use_global_device_ids=true, to_apply=%region_34.35 | all-reduce | flops 1 | bytes 8 | tf_op jit(solution)/shard_map/psum | solution.py:33
  473.1 4.7 psum.237
  477.8 10.5 %psum.238 = f32[]{:T(128)} all-reduce(f32[]{:T(128)} %psum.237), channel_id=1, replica_groups=mesh['role'=2,'gx_0'=4,'gx_1'=2,'gy_0'=4,'gy_1'=2] {'gy_0'}, use_global_device_ids=true, to_apply=%region_36.37 | all-reduce | flops 1 | bytes 8 | tf_op jit(solution)/shard_map/psum | solution.py:33
  488.3 6.7 %psum.239 = f32[]{:T(128)} all-reduce(f32[]{:T(128)} %psum.238), channel_id=1, replica_groups=mesh['role'=2,'gx_0'=4,'gx_1'=2,'gy_0'=4,'gy_1'=2] {'gy_1'}, use_global_device_ids=true, to_apply=%region_37.38 | all-reduce | flops 1 | bytes 8 | tf_op jit(solution)/shard_map/psum | solution.py:33
  514.6 8.8 %all_to_all.21 = f32[8,1,512]{2,1,0:T(1,128)S(1)} all-to-all(f32[8,1,512]{2,1,0:T(1,128)S(1)} %reshape.286), channel_id=1, replica_groups=mesh['role'=2,'gx_0'=4,'gx_1'=2,'gy_0'=4,'gy_1'=2] {'gy_0','gy_1'}, dimensions={0} | all-to-all | bytes 32768 | tf_op jit(solution)/shard_map/all_to_all | solution.py:254
  526.9 5.0 mul.384
  535.3 9.2 %collective-permute-done.28 = f32[4,256,2]{2,1,0:T(8,128)S(1)} collective-permute-done((f32[4,256,2]{2,1,0:T(8,128)S(1)}, f32[4,256,2]{2,1,0:T(8,128)S(1)}, u32[]{:S(2)}, u32[]{:S(2)}) %collective-permute-start.28) | collective-permute-done | bytes 8224 | tf_op jit(solution)/shard_map/ppermute | solution.py:23
  544.5 5.3 collective-permute-done.29
  550.4 7.0 %collective-permute-start.30 = (f32[2,256,132]{2,1,0:T(8,128)S(1)}, f32[2,256,132]{2,1,0:T(8,128)S(1)}, u32[]{:S(2)}, u32[]{:S(2)}) collective-permute-start(f32[2,256,132]{2,1,0:T(8,128)S(1)} %get-tuple-element.86), channel_id=1, source_target_pairs={{0,1},{1,2},{2,3},{3,4},{4,5},{5,6},{6,7},{7,8},{8,9},{9,10},{10,1... | collective-permute-start | bytes 811016 | tf_op jit(solution)/shard_map/ppermute | solution.py:23
  563.5 7.4 %collective-permute-done.31 = f32[2,256,132]{2,1,0:T(8,128)S(1)} collective-permute-done((f32[2,256,132]{2,1,0:T(8,128)S(1)}, f32[2,256,132]{2,1,0:T(8,128)S(1)}, u32[]{:S(2)}, u32[]{:S(2)}) %collective-permute-start.31) | collective-permute-done | bytes 270368 | tf_op jit(solution)/shard_map/ppermute | solution.py:26
  (291 shorter events, 248.7 us)
Async XLA Ops:
  0.6 111.1 %copy-start = (f32[81,81]{1,0:T(8,128)S(1)}, f32[81,81]{1,0:T(8,128)}, u32[]{:S(2)}) copy-start(f32[81,81]{1,0:T(8,128)} %param.7) | copy-start | bytes 78736
  0.6 10.6 %copy-start.20 = (s32[3,16,16,128]{3,2,1,0:T(8,128)S(1)}, s32[3,16,16,128]{3,2,1,0:T(8,128)}, u32[]{:S(2)}) copy-start(s32[3,16,16,128]{3,2,1,0:T(8,128)} %param.6) | copy-start | bytes 1179652
  0.7 10.6 %copy-start.19 = (f32[3,16,16,128]{3,2,1,0:T(8,128)S(1)}, f32[3,16,16,128]{3,2,1,0:T(8,128)}, u32[]{:S(2)}) copy-start(f32[3,16,16,128]{3,2,1,0:T(8,128)} %param.5) | copy-start | bytes 1179652
  0.7 15.4 %collective-permute-start.4 = (f32[6,17,17,1]{2,3,1,0:T(1,128)S(1)}, f32[6,17,17,1]{2,3,1,0:T(1,128)S(1)}, u32[]{:S(2)}, u32[]{:S(2)}) collective-permute-start(f32[6,17,17,1]{2,3,1,0:T(1,128)S(1)} %slice.514), channel_id=1, source_target_pairs={{0,64},{1,65},{2,66},{3,67},{4,68},{5,69},{6,70},{7,71},{8,72},{9,... | collective-permute-start | bytes 20816 | tf_op jit(solution)/shard_map/ppermute | solution.py:23
  7.9 28.1 %collective-permute-start = (f32[4,256,2]{2,1,0:T(8,128)}, f32[4,256,2]{2,1,0:T(8,128)}, u32[]{:S(2)}, u32[]{:S(2)}) collective-permute-start(f32[4,256,2]{2,1,0:T(8,128)} %get-tuple-element.92), channel_id=1, source_target_pairs={{0,64},{1,65},{2,66},{3,67},{4,68},{5,69},{6,70},{7,71},{8,72},{9,... | collective-permute-start | bytes 24584 | tf_op jit(solution)/shard_map/ppermute | solution.py:23
  10.0 26.1 %collective-permute-start.1 = (f32[4,256,2]{2,1,0:T(8,128)}, f32[4,256,2]{2,1,0:T(8,128)}, u32[]{:S(2)}, u32[]{:S(2)}) collective-permute-start(f32[4,256,2]{2,1,0:T(8,128)} %get-tuple-element.93), channel_id=1, source_target_pairs={{64,0},{65,1},{66,2},{67,3},{68,4},{69,5},{70,6},{71,7},{72,8},{73... | collective-permute-start | bytes 24584 | tf_op jit(solution)/shard_map/ppermute | solution.py:26
  14.6 12.7 %collective-permute-start.5 = (f32[6,17,17,1]{2,3,1,0:T(1,128)S(1)}, f32[6,17,17,1]{2,3,1,0:T(1,128)S(1)}, u32[]{:S(2)}, u32[]{:S(2)}) collective-permute-start(f32[6,17,17,1]{2,3,1,0:T(1,128)S(1)} %copy.52), channel_id=1, source_target_pairs={{64,0},{65,1},{66,2},{67,3},{68,4},{69,5},{70,6},{71,7},{72,8},{73... | collective-permute-start | bytes 20816 | tf_op jit(solution)/shard_map/ppermute | solution.py:26
  29.0 7.0 %copy-start.13 = (f32[4,256,128]{2,1,0:T(8,128)S(1)}, f32[4,256,128]{2,1,0:T(8,128)}, u32[]{:S(2)}) copy-start(f32[4,256,128]{2,1,0:T(8,128)} %param.4) | copy-start | bytes 1572868
  30.3 10.6 %copy-start.1 = (f32[6,17,17,1]{3,2,1,0:T(8,128)S(1)}, f32[6,17,17,1]{3,2,1,0:T(8,128)}, u32[]{:S(2)}) copy-start(f32[6,17,17,1]{3,2,1,0:T(8,128)} %copy.53) | copy-start | bytes 20812
  30.3 10.6 %copy-start.2 = (f32[6,17,17,1]{3,2,1,0:T(8,128)S(1)}, f32[6,17,17,1]{3,2,1,0:T(8,128)}, u32[]{:S(2)}) copy-start(f32[6,17,17,1]{3,2,1,0:T(8,128)} %copy.54) | copy-start | bytes 20812
  30.3 7.4 %collective-permute-start.6 = (f32[6,1,17,131]{3,2,1,0:T(8,128)S(1)}, f32[6,1,17,131]{3,2,1,0:T(8,128)S(1)}, u32[]{:S(2)}, u32[]{:S(2)}) collective-permute-start(f32[6,1,17,131]{3,2,1,0:T(8,128)S(1)} %get-tuple-element.24), channel_id=1, source_target_pairs={{0,8},{8,16},{16,24},{24,32},{32,40},{40,48},{48,56},{1,9},{9,17},... | collective-permute-start | bytes 160352 | tf_op jit(solution)/shard_map/ppermute | solution.py:23
  34.1 6.8 %collective-permute-start.7 = (f32[6,1,17,131]{3,2,1,0:T(8,128)S(1)}, f32[6,1,17,131]{3,2,1,0:T(8,128)S(1)}, u32[]{:S(2)}, u32[]{:S(2)}) collective-permute-start(f32[6,1,17,131]{3,2,1,0:T(8,128)S(1)} %get-tuple-element.25), channel_id=1, source_target_pairs={{8,0},{16,8},{24,16},{32,24},{40,32},{48,40},{56,48},{9,1},{17,9},... | collective-permute-start | bytes 160352 | tf_op jit(solution)/shard_map/ppermute | solution.py:26
  41.6 14.1 %collective-permute-start.8 = (f32[6,19,1,131]{3,2,1,0:T(1,128)S(1)}, f32[6,19,1,131]{3,2,1,0:T(1,128)S(1)}, u32[]{:S(2)}, u32[]{:S(2)}) collective-permute-start(f32[6,19,1,131]{3,2,1,0:T(1,128)S(1)} %get-tuple-element.22), channel_id=1, source_target_pairs={{0,1},{1,2},{2,3},{3,4},{4,5},{5,6},{6,7},{8,9},{9,10},{10,11},{11... | collective-permute-start | bytes 179216 | tf_op jit(solution)/shard_map/ppermute | solution.py:23
  42.9 12.8 %collective-permute-start.9 = (f32[6,19,1,131]{3,2,1,0:T(1,128)S(1)}, f32[6,19,1,131]{3,2,1,0:T(1,128)S(1)}, u32[]{:S(2)}, u32[]{:S(2)}) collective-permute-start(f32[6,19,1,131]{3,2,1,0:T(1,128)S(1)} %get-tuple-element.23), channel_id=1, source_target_pairs={{1,0},{2,1},{3,2},{4,3},{5,4},{6,5},{7,6},{9,8},{10,9},{11,10},{12... | collective-permute-start | bytes 179216 | tf_op jit(solution)/shard_map/ppermute | solution.py:26
  49.7 30.3 %collective-permute-start.2 = (f32[2,256,132]{2,1,0:T(8,128)}, f32[2,256,132]{2,1,0:T(8,128)}, u32[]{:S(2)}, u32[]{:S(2)}) collective-permute-start(f32[2,256,132]{2,1,0:T(8,128)} %get-tuple-element.88), channel_id=1, source_target_pairs={{0,1},{1,2},{2,3},{3,4},{4,5},{5,6},{6,7},{7,8},{8,9},{9,10},{10,1... | collective-permute-start | bytes 811016 | tf_op jit(solution)/shard_map/ppermute | solution.py:23
  51.6 28.4 %collective-permute-start.3 = (f32[2,256,132]{2,1,0:T(8,128)}, f32[2,256,132]{2,1,0:T(8,128)}, u32[]{:S(2)}, u32[]{:S(2)}) collective-permute-start(f32[2,256,132]{2,1,0:T(8,128)} %get-tuple-element.89), channel_id=1, source_target_pairs={{1,0},{2,1},{3,2},{4,3},{5,4},{6,5},{7,6},{8,7},{9,8},{10,9},{11,1... | collective-permute-start | bytes 811016 | tf_op jit(solution)/shard_map/ppermute | solution.py:26
  90.6 11.4 %copy-start.17 = (f32[3,3,8,8,129]{4,3,2,1,0:T(8,128)S(1)}, f32[3,3,8,8,129]{4,3,2,1,0:T(8,128)}, u32[]{:S(2)}) copy-start(f32[3,3,8,8,129]{4,3,2,1,0:T(8,128)} %slice.538) | copy-start | bytes 891652
  95.6 14.0 %all-to-all-start = ((f32[8,1,512]{2,1,0:T(1,128)}), f32[8,1,512]{2,1,0:T(1,128)S(1)}, u32[]{:S(2)}, u32[]{:S(2)}) async-start(f32[8,1,512]{2,1,0:T(1,128)} %reshape.284), calls=%async_computation | async-start | bytes 32768 | tf_op jit(solution)/shard_map/all_to_all | solution.py:222
  132.2 3.0 collective-permute-start.10
  133.9 6.1 %collective-permute-start.11 = (f32[3,17,17,1]{2,3,1,0:T(1,128)S(1)}, f32[3,17,17,1]{2,3,1,0:T(1,128)S(1)}, u32[]{:S(2)}, u32[]{:S(2)}) collective-permute-start(f32[3,17,17,1]{2,3,1,0:T(1,128)S(1)} %copy.64), channel_id=1, source_target_pairs={{64,0},{65,1},{66,2},{67,3},{68,4},{69,5},{70,6},{71,7},{72,8},{73... | collective-permute-start | bytes 10412 | tf_op jit(solution)/shard_map/ppermute | solution.py:26
  141.3 9.9 %copy-start.4 = (f32[3,8,2,17,129]{4,3,2,1,0:T(8,128)S(1)}, f32[3,8,2,17,129]{4,3,2,1,0:T(8,128)}, u32[]{:S(2)}) copy-start(f32[3,8,2,17,129]{4,3,2,1,0:T(8,128)} %copy-done.3) | copy-start | bytes 1263172
  141.3 9.9 %copy-start.10 = (f32[3,17,17,1]{3,2,1,0:T(8,128)S(1)}, f32[3,17,17,1]{3,2,1,0:T(8,128)}, u32[]{:S(2)}) copy-start(f32[3,17,17,1]{3,2,1,0:T(8,128)} %copy.66) | copy-start | bytes 10408
  142.4 5.3 collective-permute-start.12
  145.2 6.0 %collective-permute-start.13 = (f32[3,1,17,131]{3,2,1,0:T(8,128)S(1)}, f32[3,1,17,131]{3,2,1,0:T(8,128)S(1)}, u32[]{:S(2)}, u32[]{:S(2)}) collective-permute-start(f32[3,1,17,131]{3,2,1,0:T(8,128)S(1)} %get-tuple-element.38), channel_id=1, source_target_pairs={{8,0},{16,8},{24,16},{32,24},{40,32},{48,40},{56,48},{9,1},{17,9},... | collective-permute-start | bytes 80180 | tf_op jit(solution)/shard_map/ppermute | solution.py:26
  151.6 7.1 %collective-permute-start.14 = (f32[3,19,1,131]{3,2,1,0:T(1,128)S(1)}, f32[3,19,1,131]{3,2,1,0:T(1,128)S(1)}, u32[]{:S(2)}, u32[]{:S(2)}) collective-permute-start(f32[3,19,1,131]{3,2,1,0:T(1,128)S(1)} %get-tuple-element.30), channel_id=1, source_target_pairs={{0,1},{1,2},{2,3},{3,4},{4,5},{5,6},{6,7},{8,9},{9,10},{10,11},{11... | collective-permute-start | bytes 89612 | tf_op jit(solution)/shard_map/ppermute | solution.py:23
  152.9 6.6 %collective-permute-start.15 = (f32[3,19,1,131]{3,2,1,0:T(1,128)S(1)}, f32[3,19,1,131]{3,2,1,0:T(1,128)S(1)}, u32[]{:S(2)}, u32[]{:S(2)}) collective-permute-start(f32[3,19,1,131]{3,2,1,0:T(1,128)S(1)} %get-tuple-element.31), channel_id=1, source_target_pairs={{1,0},{2,1},{3,2},{4,3},{5,4},{6,5},{7,6},{9,8},{10,9},{11,10},{12... | collective-permute-start | bytes 89612 | tf_op jit(solution)/shard_map/ppermute | solution.py:26
  292.2 3.3 collective-permute-start.16
  294.2 6.1 %collective-permute-start.17 = (f32[3,17,17,1]{2,3,1,0:T(1,128)S(1)}, f32[3,17,17,1]{2,3,1,0:T(1,128)S(1)}, u32[]{:S(2)}, u32[]{:S(2)}) collective-permute-start(f32[3,17,17,1]{2,3,1,0:T(1,128)S(1)} %copy.76), channel_id=1, source_target_pairs={{64,0},{65,1},{66,2},{67,3},{68,4},{69,5},{70,6},{71,7},{72,8},{73... | collective-permute-start | bytes 10412 | tf_op jit(solution)/shard_map/ppermute | solution.py:26
  301.5 10.2 %copy-start.6 = (f32[3,8,2,17,129]{4,3,2,1,0:T(8,128)S(1)}, f32[3,8,2,17,129]{4,3,2,1,0:T(8,128)}, u32[]{:S(2)}) copy-start(f32[3,8,2,17,129]{4,3,2,1,0:T(8,128)} %copy-done.5) | copy-start | bytes 1263172
  301.5 10.2 %copy-start.11 = (f32[3,17,17,1]{3,2,1,0:T(8,128)S(1)}, f32[3,17,17,1]{3,2,1,0:T(8,128)}, u32[]{:S(2)}) copy-start(f32[3,17,17,1]{3,2,1,0:T(8,128)} %copy.78) | copy-start | bytes 10408
  302.7 5.3 collective-permute-start.18
  305.7 6.0 %collective-permute-start.19 = (f32[3,1,17,131]{3,2,1,0:T(8,128)S(1)}, f32[3,1,17,131]{3,2,1,0:T(8,128)S(1)}, u32[]{:S(2)}, u32[]{:S(2)}) collective-permute-start(f32[3,1,17,131]{3,2,1,0:T(8,128)S(1)} %get-tuple-element.36), channel_id=1, source_target_pairs={{8,0},{16,8},{24,16},{32,24},{40,32},{48,40},{56,48},{9,1},{17,9},... | collective-permute-start | bytes 80180 | tf_op jit(solution)/shard_map/ppermute | solution.py:26
  312.1 7.2 %collective-permute-start.20 = (f32[3,19,1,131]{3,2,1,0:T(1,128)S(1)}, f32[3,19,1,131]{3,2,1,0:T(1,128)S(1)}, u32[]{:S(2)}, u32[]{:S(2)}) collective-permute-start(f32[3,19,1,131]{3,2,1,0:T(1,128)S(1)} %get-tuple-element.28), channel_id=1, source_target_pairs={{0,1},{1,2},{2,3},{3,4},{4,5},{5,6},{6,7},{8,9},{9,10},{10,11},{11... | collective-permute-start | bytes 89612 | tf_op jit(solution)/shard_map/ppermute | solution.py:23
  313.4 6.6 %collective-permute-start.21 = (f32[3,19,1,131]{3,2,1,0:T(1,128)S(1)}, f32[3,19,1,131]{3,2,1,0:T(1,128)S(1)}, u32[]{:S(2)}, u32[]{:S(2)}) collective-permute-start(f32[3,19,1,131]{3,2,1,0:T(1,128)S(1)} %get-tuple-element.29), channel_id=1, source_target_pairs={{1,0},{2,1},{3,2},{4,3},{5,4},{6,5},{7,6},{9,8},{10,9},{11,10},{12... | collective-permute-start | bytes 89612 | tf_op jit(solution)/shard_map/ppermute | solution.py:26
  322.2 1.1 copy-start.16
  431.1 3.3 collective-permute-start.22
  433.1 6.1 %collective-permute-start.23 = (f32[3,17,17,1]{2,3,1,0:T(1,128)S(1)}, f32[3,17,17,1]{2,3,1,0:T(1,128)S(1)}, u32[]{:S(2)}, u32[]{:S(2)}) collective-permute-start(f32[3,17,17,1]{2,3,1,0:T(1,128)S(1)} %copy.88), channel_id=1, source_target_pairs={{64,0},{65,1},{66,2},{67,3},{68,4},{69,5},{70,6},{71,7},{72,8},{73... | collective-permute-start | bytes 10412 | tf_op jit(solution)/shard_map/ppermute | solution.py:26
  439.7 5.3 collective-permute-start.24
  442.2 6.0 %collective-permute-start.25 = (f32[3,1,17,131]{3,2,1,0:T(8,128)S(1)}, f32[3,1,17,131]{3,2,1,0:T(8,128)S(1)}, u32[]{:S(2)}, u32[]{:S(2)}) collective-permute-start(f32[3,1,17,131]{3,2,1,0:T(8,128)S(1)} %get-tuple-element.34), channel_id=1, source_target_pairs={{8,0},{16,8},{24,16},{32,24},{40,32},{48,40},{56,48},{9,1},{17,9},... | collective-permute-start | bytes 80180 | tf_op jit(solution)/shard_map/ppermute | solution.py:26
  448.7 7.3 %collective-permute-start.26 = (f32[3,19,1,131]{3,2,1,0:T(1,128)S(1)}, f32[3,19,1,131]{3,2,1,0:T(1,128)S(1)}, u32[]{:S(2)}, u32[]{:S(2)}) collective-permute-start(f32[3,19,1,131]{3,2,1,0:T(1,128)S(1)} %get-tuple-element.26), channel_id=1, source_target_pairs={{0,1},{1,2},{2,3},{3,4},{4,5},{5,6},{6,7},{8,9},{9,10},{10,11},{11... | collective-permute-start | bytes 89612 | tf_op jit(solution)/shard_map/ppermute | solution.py:23
  450.0 6.6 %collective-permute-start.27 = (f32[3,19,1,131]{3,2,1,0:T(1,128)S(1)}, f32[3,19,1,131]{3,2,1,0:T(1,128)S(1)}, u32[]{:S(2)}, u32[]{:S(2)}) collective-permute-start(f32[3,19,1,131]{3,2,1,0:T(1,128)S(1)} %get-tuple-element.27), channel_id=1, source_target_pairs={{1,0},{2,1},{3,2},{4,3},{5,4},{6,5},{7,6},{9,8},{10,9},{11,10},{12... | collective-permute-start | bytes 89612 | tf_op jit(solution)/shard_map/ppermute | solution.py:26
  457.8 38.6 %copy-start.7 = (f32[3,17,17,129]{3,2,1,0:T(8,128)S(1)}, f32[3,17,17,129]{3,2,1,0:T(8,128)}, u32[]{:S(2)}) copy-start(f32[3,17,17,129]{3,2,1,0:T(8,128)} %get-tuple-element.21) | copy-start | bytes 1342120
  457.8 38.6 %copy-start.8 = (f32[3,17,17,129]{3,2,1,0:T(8,128)S(1)}, f32[3,17,17,129]{3,2,1,0:T(8,128)}, u32[]{:S(2)}) copy-start(f32[3,17,17,129]{3,2,1,0:T(8,128)} %get-tuple-element.17) | copy-start | bytes 1342120
  526.9 5.1 copy-start.18
  532.4 12.1 %collective-permute-start.28 = (f32[4,256,2]{2,1,0:T(8,128)S(1)}, f32[4,256,2]{2,1,0:T(8,128)S(1)}, u32[]{:S(2)}, u32[]{:S(2)}) collective-permute-start(f32[4,256,2]{2,1,0:T(8,128)S(1)} %get-tuple-element.90), channel_id=1, source_target_pairs={{0,64},{1,65},{2,66},{3,67},{4,68},{5,69},{6,70},{7,71},{8,72},{9,... | collective-permute-start | bytes 24584 | tf_op jit(solution)/shard_map/ppermute | solution.py:23
  534.0 15.8 %collective-permute-start.29 = (f32[4,256,2]{2,1,0:T(8,128)S(1)}, f32[4,256,2]{2,1,0:T(8,128)S(1)}, u32[]{:S(2)}, u32[]{:S(2)}) collective-permute-start(f32[4,256,2]{2,1,0:T(8,128)S(1)} %get-tuple-element.91), channel_id=1, source_target_pairs={{64,0},{65,1},{66,2},{67,3},{68,4},{69,5},{70,6},{71,7},{72,8},{73... | collective-permute-start | bytes 24584 | tf_op jit(solution)/shard_map/ppermute | solution.py:26
  550.4 13.1 %collective-permute-start.30 = (f32[2,256,132]{2,1,0:T(8,128)S(1)}, f32[2,256,132]{2,1,0:T(8,128)S(1)}, u32[]{:S(2)}, u32[]{:S(2)}) collective-permute-start(f32[2,256,132]{2,1,0:T(8,128)S(1)} %get-tuple-element.86), channel_id=1, source_target_pairs={{0,1},{1,2},{2,3},{3,4},{4,5},{5,6},{6,7},{7,8},{8,9},{9,10},{10,1... | collective-permute-start | bytes 811016 | tf_op jit(solution)/shard_map/ppermute | solution.py:23
  557.4 13.5 %collective-permute-start.31 = (f32[2,256,132]{2,1,0:T(8,128)S(1)}, f32[2,256,132]{2,1,0:T(8,128)S(1)}, u32[]{:S(2)}, u32[]{:S(2)}) collective-permute-start(f32[2,256,132]{2,1,0:T(8,128)S(1)} %get-tuple-element.87), channel_id=1, source_target_pairs={{1,0},{2,1},{3,2},{4,3},{5,4},{6,5},{7,6},{8,7},{9,8},{10,9},{11,1... | collective-permute-start | bytes 811016 | tf_op jit(solution)/shard_map/ppermute | solution.py:26
  (6 other events, 6.3 us)
where the time goes:
time: 581 us; the launch traced here: 574 us
  blocking collectives  187 us (32%)
  local copies, waits for them, and re-layouts  131 us (23%)
  starting transfers between devices  92 us (16%)
  waiting for transfers between devices  62.5 us (11%)
  other arithmetic  52.8 us (9%)
  matrix products  40.7 us (7%)
  between operations  9 us (2%)
    psum x25, blocking collectives, over_axes(): shard = lax.psum(shard, axis)  178 us
    ppermute x16, waiting for transfers between devices, with_halo(): lax.ppermute(lax.slice_in_dim(block, 0, width, axis=dim), axis, backward)  50.9 us
    slice x12, local copies, waits for them, and re-layouts, split_axis(): lax.slice_in_dim(values, corner, corner + 2 * half_len - 1, stride=2, axi...  47.5 us
    ppermute x16, starting transfers between devices, with_halo(): lax.ppermute(lax.slice_in_dim(block, 0, width, axis=dim), axis, backward)  46.6 us
    ppermute x16, starting transfers between devices, with_halo(): lax.ppermute(lax.slice_in_dim(block, block.shape[dim] - width, None, axis...  39 us
    dot_general x4, matrix products, split_nodes(): jnp.einsum('baqxyk,ckg->cbaqxyg', stacked, table, precision=lax.Precision...  14.6 us
    unnamed x54, local copies, waits for them, and re-layouts  12.2 us
    ppermute x16, waiting for transfers between devices, with_halo(): lax.ppermute(lax.slice_in_dim(block, block.shape[dim] - width, None, axis...  11.6 us
  transfers between devices with their start and end apart: 33, of which 15 were waited for; matrix products, arithmetic and copies ran while one was open for 9% of the time, Pallas kernels for 0%

commit v1 on v0

--- a/solution.py
+++ b/solution.py
@@ -30,7 +30,7 @@
 
 def over_axes(shard, axes):
     for axis in axes:
-        shard = lax.psum(shard, axis)
+        shard = jax.lax.all_gather(shard, axis).sum(axis=0)
     return shard
 
 

time: 581 us -> 625 us (1.076)
  local copies, waits for them, and re-layouts: 131 us -> 173 us
  waiting for transfers between devices: 62.5 us -> 29.7 us
  starting transfers between devices: 92 us -> 114 us
  other arithmetic: 52.8 us -> 73.1 us
  blocking collectives: 187 us -> 173 us
    psum x25 -> x0, blocking collectives: 178 us -> none  [over_axes(): shard = lax.psum(shard, axis)]
    unnamed x0 -> x25, blocking collectives: none -> 164 us
    unnamed x54 -> x117, local copies, waits for them, and re-layouts: 12.2 us -> 57.6 us
    ppermute x16, waiting for transfers between devices: 50.9 us -> 12.5 us  [with_halo(): lax.ppermute(lax.slice_in_dim(block, 0, width, axis=dim), axis, backward)]
    ppermute x16, starting transfers between devices: 39 us -> 66.2 us  [with_halo(): lax.ppermute(lax.slice_in_dim(block, block.shape[dim] - width, None, axis...]
    reduce_sum x0 -> x30, other arithmetic: none -> 18.2 us  [over_axes(): shard = jax.lax.all_gather(shard, axis).sum(axis=0)]
  transfers between devices with their start and end apart: 33 -> 33, of which waited for: 15 -> 14; matrix products, arithmetic and copies ran while one was open for 9% -> 8% of each run, Pallas kernels for 0% -> 0%
where the time goes in v1:
time: 625 us; the launch traced here: 614 us
  local copies, waits for them, and re-layouts  173 us (28%)
  blocking collectives  173 us (28%)
  starting transfers between devices  114 us (18%)
  other arithmetic  73.1 us (12%)
  matrix products  41.9 us (7%)
  waiting for transfers between devices  29.7 us (5%)
  between operations  9.15 us (1%)
    unnamed x25, blocking collectives  164 us
    ppermute x16, starting transfers between devices, with_halo(): lax.ppermute(lax.slice_in_dim(block, block.shape[dim] - width, None, axis...  66.2 us
    unnamed x117, local copies, waits for them, and re-layouts  57.6 us
    ppermute x16, starting transfers between devices, with_halo(): lax.ppermute(lax.slice_in_dim(block, 0, width, axis=dim), axis, backward)  43.5 us
    slice x12, local copies, waits for them, and re-layouts, split_axis(): lax.slice_in_dim(values, corner, corner + 2 * half_len - 1, stride=2, axi...  41.9 us
    reduce_sum x30, other arithmetic, over_axes(): shard = jax.lax.all_gather(shard, axis).sum(axis=0)  18.2 us
    ppermute x16, waiting for transfers between devices, with_halo(): lax.ppermute(lax.slice_in_dim(block, block.shape[dim] - width, None, axis...  17.2 us
    dot_general x4, matrix products, split_nodes(): jnp.einsum('baqxyk,ckg->cbaqxyg', stacked, table, precision=lax.Precision...  17.1 us
  transfers between devices with their start and end apart: 33, of which 14 were waited for; matrix products, arithmetic and copies ran while one was open for 8% of the time, Pallas kernels for 0%

profile of v1, /device:TPU:39, one launch (start us, length us, event | category | flops | bytes accessed | tf_op | source)
XLA Modules:
  0.0 613.8 jit_solution(14274410766484871311)
XLA Ops:
  4.3 7.1 %collective-permute-start = (f32[4,256,2]{2,1,0:T(8,128)}, f32[4,256,2]{2,1,0:T(8,128)}, u32[]{:S(2)}, u32[]{:S(2)}) collective-permute-start(f32[4,256,2]{2,1,0:T(8,128)} %get-tuple-element.92), channel_id=1, source_target_pairs={{0,64},{1,65},{2,66},{3,67},{4,68},{5,69},{6,70},{7,71},{8,72},{9,... | collective-permute-start | bytes 24584 | tf_op jit(solution)/shard_map/ppermute | solution.py:23
  16.1 5.5 collective-permute-start.4
  47.0 6.1 collective-permute-start.2
  60.2 5.8 slice.538
  66.0 5.7 slice.537
  71.6 5.7 slice.536
  82.2 5.7 reduce_sum.350
  92.9 4.5 all-to-all-start
  97.4 4.4 fusion.40
  129.4 5.5 collective-permute-start.10
  146.9 5.1 collective-permute-start.15
  165.2 5.8 all-reduce.49
  175.7 8.5 %all-reduce.46 = (f32[4]{0:T(128)S(1)}, f32[4]{0:T(128)S(1)}) all-reduce(f32[4]{0:T(128)S(1)} %dynamic-update-slice.1, f32[4]{0:T(128)S(1)} %dynamic-update-slice.6), channel_id=1, replica_groups=mesh['role'=2,'gx_0'=4,'gx_1'=2,'gy_0'=4,'gy_1'=2] {'gx_0'}, use_global_device_ids=true, to_apply=%add.16 | all-reduce | flops 8 | bytes 64
  188.7 5.4 all-reduce.48
  198.8 5.7 all-reduce.45
  208.6 9.3 %all-reduce.47 = (f32[2]{0:T(128)S(1)}, f32[2]{0:T(128)S(1)}) all-reduce(f32[2]{0:T(128)S(1)} %dynamic-update-slice.4, f32[2]{0:T(128)S(1)} %dynamic-update-slice.9), channel_id=1, replica_groups=mesh['role'=2,'gx_0'=4,'gx_1'=2,'gy_0'=4,'gy_1'=2] {'gy_1'}, use_global_device_ids=true, to_apply=%add.19 | all-reduce | flops 4 | bytes 32
  225.3 5.3 all-reduce.25
  232.6 6.0 all-reduce.26
  240.5 4.3 all-reduce.27
  246.7 8.0 %all-reduce.28 = f32[4]{0:T(128)S(1)} all-reduce(f32[4]{0:T(128)S(1)} %dynamic-update-slice.13), channel_id=1, replica_groups=mesh['role'=2,'gx_0'=4,'gx_1'=2,'gy_0'=4,'gy_1'=2] {'gy_0'}, use_global_device_ids=true, to_apply=%add.28 | all-reduce | flops 4 | bytes 32
  256.7 8.3 %all-reduce.29 = f32[2]{0:T(128)S(1)} all-reduce(f32[2]{0:T(128)S(1)} %dynamic-update-slice.14), channel_id=1, replica_groups=mesh['role'=2,'gx_0'=4,'gx_1'=2,'gy_0'=4,'gy_1'=2] {'gy_1'}, use_global_device_ids=true, to_apply=%add.29 | all-reduce | flops 2 | bytes 16
  272.1 4.9 slice.572
  277.0 5.7 slice.571
  282.7 5.7 slice.570
  288.4 4.4 fusion.39
  318.4 5.5 collective-permute-start.16
  336.9 4.3 collective-permute-start.21
  350.6 5.3 all-reduce.30
  357.9 7.7 %all-reduce.31 = f32[4]{0:T(128)S(1)} all-reduce(f32[4]{0:T(128)S(1)} %dynamic-update-slice.16), channel_id=1, replica_groups=mesh['role'=2,'gx_0'=4,'gx_1'=2,'gy_0'=4,'gy_1'=2] {'gx_0'}, use_global_device_ids=true, to_apply=%add.31 | all-reduce | flops 4 | bytes 32
  373.4 7.3 %all-reduce.33 = f32[4]{0:T(128)S(1)} all-reduce(f32[4]{0:T(128)S(1)} %dynamic-update-slice.18), channel_id=1, replica_groups=mesh['role'=2,'gx_0'=4,'gx_1'=2,'gy_0'=4,'gy_1'=2] {'gy_0'}, use_global_device_ids=true, to_apply=%add.33 | all-reduce | flops 4 | bytes 32
  382.8 9.0 %all-reduce.34 = f32[2]{0:T(128)S(1)} all-reduce(f32[2]{0:T(128)S(1)} %dynamic-update-slice.19), channel_id=1, replica_groups=mesh['role'=2,'gx_0'=4,'gx_1'=2,'gy_0'=4,'gy_1'=2] {'gy_1'}, use_global_device_ids=true, to_apply=%add.34 | all-reduce | flops 2 | bytes 16
  398.6 5.3 all-reduce.35
  405.9 6.2 %all-reduce.36 = f32[4]{0:T(128)S(1)} all-reduce(f32[4]{0:T(128)S(1)} %dynamic-update-slice.21), channel_id=1, replica_groups=mesh['role'=2,'gx_0'=4,'gx_1'=2,'gy_0'=4,'gy_1'=2] {'gx_0'}, use_global_device_ids=true, to_apply=%add.36 | all-reduce | flops 4 | bytes 32
  414.2 4.3 all-reduce.37
  420.5 7.9 %all-reduce.38 = f32[4]{0:T(128)S(1)} all-reduce(f32[4]{0:T(128)S(1)} %dynamic-update-slice.23), channel_id=1, replica_groups=mesh['role'=2,'gx_0'=4,'gx_1'=2,'gy_0'=4,'gy_1'=2] {'gy_0'}, use_global_device_ids=true, to_apply=%add.38 | all-reduce | flops 4 | bytes 32
  430.4 8.2 %all-reduce.39 = f32[2]{0:T(128)S(1)} all-reduce(f32[2]{0:T(128)S(1)} %dynamic-update-slice.24), channel_id=1, replica_groups=mesh['role'=2,'gx_0'=4,'gx_1'=2,'gy_0'=4,'gy_1'=2] {'gy_1'}, use_global_device_ids=true, to_apply=%add.39 | all-reduce | flops 2 | bytes 16
  472.9 5.5 collective-permute-start.22
  489.0 4.8 collective-permute-start.27
  502.4 5.3 all-reduce.40
  509.6 6.3 %all-reduce.41 = f32[4]{0:T(128)S(1)} all-reduce(f32[4]{0:T(128)S(1)} %dynamic-update-slice.26), channel_id=1, replica_groups=mesh['role'=2,'gx_0'=4,'gx_1'=2,'gy_0'=4,'gy_1'=2] {'gx_0'}, use_global_device_ids=true, to_apply=%add.41 | all-reduce | flops 4 | bytes 32
  517.8 4.9 all-reduce.42
  524.6 7.5 %all-reduce.43 = f32[4]{0:T(128)S(1)} all-reduce(f32[4]{0:T(128)S(1)} %dynamic-update-slice.28), channel_id=1, replica_groups=mesh['role'=2,'gx_0'=4,'gx_1'=2,'gy_0'=4,'gy_1'=2] {'gy_0'}, use_global_device_ids=true, to_apply=%add.43 | all-reduce | flops 4 | bytes 32
  534.0 8.3 %all-reduce.44 = f32[2]{0:T(128)S(1)} all-reduce(f32[2]{0:T(128)S(1)} %dynamic-update-slice.29), channel_id=1, replica_groups=mesh['role'=2,'gx_0'=4,'gx_1'=2,'gy_0'=4,'gy_1'=2] {'gy_1'}, use_global_device_ids=true, to_apply=%add.44 | all-reduce | flops 2 | bytes 16
  559.5 8.7 %all_to_all.21 = f32[8,1,512]{2,1,0:T(1,128)S(1)} all-to-all(f32[8,1,512]{2,1,0:T(1,128)S(1)} %reshape.436), channel_id=1, replica_groups=mesh['role'=2,'gx_0'=4,'gx_1'=2,'gy_0'=4,'gy_1'=2] {'gy_0','gy_1'}, dimensions={0} | all-to-all | bytes 32768 | tf_op jit(solution)/shard_map/all_to_all | solution.py:254
  571.7 5.0 mul.384
  578.5 5.6 collective-permute-start.28
  584.1 9.3 %collective-permute-done.29 = f32[4,256,2]{2,1,0:T(8,128)S(1)} collective-permute-done((f32[4,256,2]{2,1,0:T(8,128)S(1)}, f32[4,256,2]{2,1,0:T(8,128)S(1)}, u32[]{:S(2)}, u32[]{:S(2)}) %collective-permute-start.29) | collective-permute-done | bytes 8224 | tf_op jit(solution)/shard_map/ppermute | solution.py:26
  598.9 5.4 collective-permute-start.30
  (396 shorter events, 309.1 us)
Async XLA Ops:
  0.6 106.5 %copy-start = (f32[81,81]{1,0:T(8,128)S(1)}, f32[81,81]{1,0:T(8,128)}, u32[]{:S(2)}) copy-start(f32[81,81]{1,0:T(8,128)} %param.7) | copy-start | bytes 78736
  0.6 10.8 %copy-start.20 = (s32[3,16,16,128]{3,2,1,0:T(8,128)S(1)}, s32[3,16,16,128]{3,2,1,0:T(8,128)}, u32[]{:S(2)}) copy-start(s32[3,16,16,128]{3,2,1,0:T(8,128)} %param.6) | copy-start | bytes 1179652
  0.7 10.8 %copy-start.19 = (f32[3,16,16,128]{3,2,1,0:T(8,128)S(1)}, f32[3,16,16,128]{3,2,1,0:T(8,128)}, u32[]{:S(2)}) copy-start(f32[3,16,16,128]{3,2,1,0:T(8,128)} %param.5) | copy-start | bytes 1179652
  3.1 29.9 %collective-permute-start.1 = (f32[4,256,2]{2,1,0:T(8,128)}, f32[4,256,2]{2,1,0:T(8,128)}, u32[]{:S(2)}, u32[]{:S(2)}) collective-permute-start(f32[4,256,2]{2,1,0:T(8,128)} %get-tuple-element.93), channel_id=1, source_target_pairs={{64,0},{65,1},{66,2},{67,3},{68,4},{69,5},{70,6},{71,7},{72,8},{73... | collective-permute-start | bytes 24584 | tf_op jit(solution)/shard_map/ppermute | solution.py:26
  4.3 28.6 %collective-permute-start = (f32[4,256,2]{2,1,0:T(8,128)}, f32[4,256,2]{2,1,0:T(8,128)}, u32[]{:S(2)}, u32[]{:S(2)}) collective-permute-start(f32[4,256,2]{2,1,0:T(8,128)} %get-tuple-element.92), channel_id=1, source_target_pairs={{0,64},{1,65},{2,66},{3,67},{4,68},{5,69},{6,70},{7,71},{8,72},{9,... | collective-permute-start | bytes 24584 | tf_op jit(solution)/shard_map/ppermute | solution.py:23
  14.8 7.0 %collective-permute-start.5 = (f32[6,17,17,1]{2,3,1,0:T(1,128)S(1)}, f32[6,17,17,1]{2,3,1,0:T(1,128)S(1)}, u32[]{:S(2)}, u32[]{:S(2)}) collective-permute-start(f32[6,17,17,1]{2,3,1,0:T(1,128)S(1)} %copy.52), channel_id=1, source_target_pairs={{64,0},{65,1},{66,2},{67,3},{68,4},{69,5},{70,6},{71,7},{72,8},{73... | collective-permute-start | bytes 20816 | tf_op jit(solution)/shard_map/ppermute | solution.py:26
  16.1 7.4 %collective-permute-start.4 = (f32[6,17,17,1]{2,3,1,0:T(1,128)S(1)}, f32[6,17,17,1]{2,3,1,0:T(1,128)S(1)}, u32[]{:S(2)}, u32[]{:S(2)}) collective-permute-start(f32[6,17,17,1]{2,3,1,0:T(1,128)S(1)} %slice.514), channel_id=1, source_target_pairs={{0,64},{1,65},{2,66},{3,67},{4,68},{5,69},{6,70},{7,71},{8,72},{9,... | collective-permute-start | bytes 20816 | tf_op jit(solution)/shard_map/ppermute | solution.py:23
  26.6 11.1 %copy-start.1 = (f32[6,17,17,1]{3,2,1,0:T(8,128)S(1)}, f32[6,17,17,1]{3,2,1,0:T(8,128)}, u32[]{:S(2)}) copy-start(f32[6,17,17,1]{3,2,1,0:T(8,128)} %copy.54) | copy-start | bytes 20812
  26.6 11.1 %copy-start.2 = (f32[6,17,17,1]{3,2,1,0:T(8,128)S(1)}, f32[6,17,17,1]{3,2,1,0:T(8,128)}, u32[]{:S(2)}) copy-start(f32[6,17,17,1]{3,2,1,0:T(8,128)} %copy.53) | copy-start | bytes 20812
  26.6 8.1 %collective-permute-start.7 = (f32[6,1,17,131]{3,2,1,0:T(8,128)S(1)}, f32[6,1,17,131]{3,2,1,0:T(8,128)S(1)}, u32[]{:S(2)}, u32[]{:S(2)}) collective-permute-start(f32[6,1,17,131]{3,2,1,0:T(8,128)S(1)} %get-tuple-element.25), channel_id=1, source_target_pairs={{8,0},{16,8},{24,16},{32,24},{40,32},{48,40},{56,48},{9,1},{17,9},... | collective-permute-start | bytes 160352 | tf_op jit(solution)/shard_map/ppermute | solution.py:26
  28.7 9.0 %collective-permute-start.6 = (f32[6,1,17,131]{3,2,1,0:T(8,128)S(1)}, f32[6,1,17,131]{3,2,1,0:T(8,128)S(1)}, u32[]{:S(2)}, u32[]{:S(2)}) collective-permute-start(f32[6,1,17,131]{3,2,1,0:T(8,128)S(1)} %get-tuple-element.24), channel_id=1, source_target_pairs={{0,8},{8,16},{16,24},{24,32},{32,40},{40,48},{48,56},{1,9},{9,17},... | collective-permute-start | bytes 160352 | tf_op jit(solution)/shard_map/ppermute | solution.py:23
  38.4 14.6 %collective-permute-start.9 = (f32[6,19,1,131]{3,2,1,0:T(1,128)S(1)}, f32[6,19,1,131]{3,2,1,0:T(1,128)S(1)}, u32[]{:S(2)}, u32[]{:S(2)}) collective-permute-start(f32[6,19,1,131]{3,2,1,0:T(1,128)S(1)} %get-tuple-element.23), channel_id=1, source_target_pairs={{1,0},{2,1},{3,2},{4,3},{5,4},{6,5},{7,6},{9,8},{10,9},{11,10},{12... | collective-permute-start | bytes 179216 | tf_op jit(solution)/shard_map/ppermute | solution.py:26
  41.6 11.5 %collective-permute-start.8 = (f32[6,19,1,131]{3,2,1,0:T(1,128)S(1)}, f32[6,19,1,131]{3,2,1,0:T(1,128)S(1)}, u32[]{:S(2)}, u32[]{:S(2)}) collective-permute-start(f32[6,19,1,131]{3,2,1,0:T(1,128)S(1)} %get-tuple-element.22), channel_id=1, source_target_pairs={{0,1},{1,2},{2,3},{3,4},{4,5},{5,6},{6,7},{8,9},{9,10},{10,11},{11... | collective-permute-start | bytes 179216 | tf_op jit(solution)/shard_map/ppermute | solution.py:23
  43.9 33.4 %collective-permute-start.3 = (f32[2,256,132]{2,1,0:T(8,128)}, f32[2,256,132]{2,1,0:T(8,128)}, u32[]{:S(2)}, u32[]{:S(2)}) collective-permute-start(f32[2,256,132]{2,1,0:T(8,128)} %get-tuple-element.89), channel_id=1, source_target_pairs={{1,0},{2,1},{3,2},{4,3},{5,4},{6,5},{7,6},{8,7},{9,8},{10,9},{11,1... | collective-permute-start | bytes 811016 | tf_op jit(solution)/shard_map/ppermute | solution.py:26
  47.0 30.3 %collective-permute-start.2 = (f32[2,256,132]{2,1,0:T(8,128)}, f32[2,256,132]{2,1,0:T(8,128)}, u32[]{:S(2)}, u32[]{:S(2)}) collective-permute-start(f32[2,256,132]{2,1,0:T(8,128)} %get-tuple-element.88), channel_id=1, source_target_pairs={{0,1},{1,2},{2,3},{3,4},{4,5},{5,6},{6,7},{7,8},{8,9},{9,10},{10,1... | collective-permute-start | bytes 811016 | tf_op jit(solution)/shard_map/ppermute | solution.py:23
  87.9 9.5 %copy-start.17 = (f32[3,3,8,8,129]{4,3,2,1,0:T(8,128)S(1)}, f32[3,3,8,8,129]{4,3,2,1,0:T(8,128)}, u32[]{:S(2)}) copy-start(f32[3,3,8,8,129]{4,3,2,1,0:T(8,128)} %slice.538) | copy-start | bytes 891652
  92.9 12.1 %all-to-all-start = ((f32[8,1,512]{2,1,0:T(1,128)}), f32[8,1,512]{2,1,0:T(1,128)S(1)}, u32[]{:S(2)}, u32[]{:S(2)}) async-start(f32[8,1,512]{2,1,0:T(1,128)} %reshape.434), calls=%async_computation | async-start | bytes 32768 | tf_op jit(solution)/shard_map/all_to_all | solution.py:222
  127.7 7.2 %collective-permute-start.11 = (f32[3,17,17,1]{2,3,1,0:T(1,128)S(1)}, f32[3,17,17,1]{2,3,1,0:T(1,128)S(1)}, u32[]{:S(2)}, u32[]{:S(2)}) collective-permute-start(f32[3,17,17,1]{2,3,1,0:T(1,128)S(1)} %copy.64), channel_id=1, source_target_pairs={{64,0},{65,1},{66,2},{67,3},{68,4},{69,5},{70,6},{71,7},{72,8},{73... | collective-permute-start | bytes 10412 | tf_op jit(solution)/shard_map/ppermute | solution.py:26
  129.4 6.4 %collective-permute-start.10 = (f32[3,17,17,1]{2,3,1,0:T(1,128)S(1)}, f32[3,17,17,1]{2,3,1,0:T(1,128)S(1)}, u32[]{:S(2)}, u32[]{:S(2)}) collective-permute-start(f32[3,17,17,1]{2,3,1,0:T(1,128)S(1)} %copy.63), channel_id=1, source_target_pairs={{0,64},{1,65},{2,66},{3,67},{4,68},{5,69},{6,70},{7,71},{8,72},{9,... | collective-permute-start | bytes 10412 | tf_op jit(solution)/shard_map/ppermute | solution.py:23
  137.1 8.8 %copy-start.10 = (f32[3,17,17,1]{3,2,1,0:T(8,128)S(1)}, f32[3,17,17,1]{3,2,1,0:T(8,128)}, u32[]{:S(2)}) copy-start(f32[3,17,17,1]{3,2,1,0:T(8,128)} %copy.65) | copy-start | bytes 10408
  138.3 15.3 %copy-start.25 = (u32[128]{0:T(128)S(1)}, u32[128]{0:T(128)}, u32[]{:S(2)}) copy-start(u32[128]{0:T(128)} %constant.144) | copy-start | bytes 1540
  138.3 6.2 %collective-permute-start.13 = (f32[3,1,17,131]{3,2,1,0:T(8,128)S(1)}, f32[3,1,17,131]{3,2,1,0:T(8,128)S(1)}, u32[]{:S(2)}, u32[]{:S(2)}) collective-permute-start(f32[3,1,17,131]{3,2,1,0:T(8,128)S(1)} %get-tuple-element.38), channel_id=1, source_target_pairs={{8,0},{16,8},{24,16},{32,24},{40,32},{48,40},{56,48},{9,1},{17,9},... | collective-permute-start | bytes 80180 | tf_op jit(solution)/shard_map/ppermute | solution.py:26
  140.2 5.7 collective-permute-start.12
  146.9 7.2 %collective-permute-start.15 = (f32[3,19,1,131]{3,2,1,0:T(1,128)}, f32[3,19,1,131]{3,2,1,0:T(1,128)}, u32[]{:S(2)}, u32[]{:S(2)}) collective-permute-start(f32[3,19,1,131]{3,2,1,0:T(1,128)} %get-tuple-element.31), channel_id=1, source_target_pairs={{1,0},{2,1},{3,2},{4,3},{5,4},{6,5},{7,6},{9,8},{10,9},{11,10},{12... | collective-permute-start | bytes 89612 | tf_op jit(solution)/shard_map/ppermute | solution.py:26
  152.0 3.3 collective-permute-start.14
  157.9 17.2 %copy-start.23 = (u32[128]{0:T(128)S(1)}, u32[128]{0:T(128)}, u32[]{:S(2)}) copy-start(u32[128]{0:T(128)} %constant.154) | copy-start | bytes 1540
  158.0 30.2 %copy-start.22 = (u32[128]{0:T(128)S(1)}, u32[128]{0:T(128)}, u32[]{:S(2)}) copy-start(u32[128]{0:T(128)} %constant.159) | copy-start | bytes 1540
  158.0 40.2 %copy-start.21 = (u32[128]{0:T(128)S(1)}, u32[128]{0:T(128)}, u32[]{:S(2)}) copy-start(u32[128]{0:T(128)} %constant.164) | copy-start | bytes 1540
  316.7 7.2 %collective-permute-start.17 = (f32[3,17,17,1]{2,3,1,0:T(1,128)S(1)}, f32[3,17,17,1]{2,3,1,0:T(1,128)S(1)}, u32[]{:S(2)}, u32[]{:S(2)}) collective-permute-start(f32[3,17,17,1]{2,3,1,0:T(1,128)S(1)} %copy.76), channel_id=1, source_target_pairs={{64,0},{65,1},{66,2},{67,3},{68,4},{69,5},{70,6},{71,7},{72,8},{73... | collective-permute-start | bytes 10412 | tf_op jit(solution)/shard_map/ppermute | solution.py:26
  318.4 6.4 %collective-permute-start.16 = (f32[3,17,17,1]{2,3,1,0:T(1,128)S(1)}, f32[3,17,17,1]{2,3,1,0:T(1,128)S(1)}, u32[]{:S(2)}, u32[]{:S(2)}) collective-permute-start(f32[3,17,17,1]{2,3,1,0:T(1,128)S(1)} %copy.75), channel_id=1, source_target_pairs={{0,64},{1,65},{2,66},{3,67},{4,68},{5,69},{6,70},{7,71},{8,72},{9,... | collective-permute-start | bytes 10412 | tf_op jit(solution)/shard_map/ppermute | solution.py:23
  326.0 10.5 %copy-start.6 = (f32[3,8,2,17,129]{4,3,2,1,0:T(8,128)S(1)}, f32[3,8,2,17,129]{4,3,2,1,0:T(8,128)}, u32[]{:S(2)}) copy-start(f32[3,8,2,17,129]{4,3,2,1,0:T(8,128)} %copy-done.5) | copy-start | bytes 1263172
  326.0 10.5 %copy-start.11 = (f32[3,17,17,1]{3,2,1,0:T(8,128)S(1)}, f32[3,17,17,1]{3,2,1,0:T(8,128)}, u32[]{:S(2)}) copy-start(f32[3,17,17,1]{3,2,1,0:T(8,128)} %copy.77) | copy-start | bytes 10408
  327.2 7.1 %collective-permute-start.19 = (f32[3,1,17,131]{3,2,1,0:T(8,128)S(1)}, f32[3,1,17,131]{3,2,1,0:T(8,128)S(1)}, u32[]{:S(2)}, u32[]{:S(2)}) collective-permute-start(f32[3,1,17,131]{3,2,1,0:T(8,128)S(1)} %get-tuple-element.36), channel_id=1, source_target_pairs={{8,0},{16,8},{24,16},{32,24},{40,32},{48,40},{56,48},{9,1},{17,9},... | collective-permute-start | bytes 80180 | tf_op jit(solution)/shard_map/ppermute | solution.py:26
  330.9 5.6 collective-permute-start.18
  336.9 5.8 collective-permute-start.21
  341.2 3.1 collective-permute-start.20
  471.2 7.2 %collective-permute-start.23 = (f32[3,17,17,1]{2,3,1,0:T(1,128)S(1)}, f32[3,17,17,1]{2,3,1,0:T(1,128)S(1)}, u32[]{:S(2)}, u32[]{:S(2)}) collective-permute-start(f32[3,17,17,1]{2,3,1,0:T(1,128)S(1)} %copy.88), channel_id=1, source_target_pairs={{64,0},{65,1},{66,2},{67,3},{68,4},{69,5},{70,6},{71,7},{72,8},{73... | collective-permute-start | bytes 10412 | tf_op jit(solution)/shard_map/ppermute | solution.py:26
  472.9 6.4 %collective-permute-start.22 = (f32[3,17,17,1]{2,3,1,0:T(1,128)S(1)}, f32[3,17,17,1]{2,3,1,0:T(1,128)S(1)}, u32[]{:S(2)}, u32[]{:S(2)}) collective-permute-start(f32[3,17,17,1]{2,3,1,0:T(1,128)S(1)} %copy.87), channel_id=1, source_target_pairs={{0,64},{1,65},{2,66},{3,67},{4,68},{5,69},{6,70},{7,71},{8,72},{9,... | collective-permute-start | bytes 10412 | tf_op jit(solution)/shard_map/ppermute | solution.py:23
  479.9 6.2 %collective-permute-start.25 = (f32[3,1,17,131]{3,2,1,0:T(8,128)S(1)}, f32[3,1,17,131]{3,2,1,0:T(8,128)S(1)}, u32[]{:S(2)}, u32[]{:S(2)}) collective-permute-start(f32[3,1,17,131]{3,2,1,0:T(8,128)S(1)} %get-tuple-element.34), channel_id=1, source_target_pairs={{8,0},{16,8},{24,16},{32,24},{40,32},{48,40},{56,48},{9,1},{17,9},... | collective-permute-start | bytes 80180 | tf_op jit(solution)/shard_map/ppermute | solution.py:26
  483.5 5.1 collective-permute-start.24
  489.0 6.3 %collective-permute-start.27 = (f32[3,19,1,131]{3,2,1,0:T(1,128)S(1)}, f32[3,19,1,131]{3,2,1,0:T(1,128)S(1)}, u32[]{:S(2)}, u32[]{:S(2)}) collective-permute-start(f32[3,19,1,131]{3,2,1,0:T(1,128)S(1)} %get-tuple-element.27), channel_id=1, source_target_pairs={{1,0},{2,1},{3,2},{4,3},{5,4},{6,5},{7,6},{9,8},{10,9},{11,10},{12... | collective-permute-start | bytes 89612 | tf_op jit(solution)/shard_map/ppermute | solution.py:26
  493.8 3.1 collective-permute-start.26
  498.2 46.0 %copy-start.7 = (f32[3,17,17,129]{3,2,1,0:T(8,128)S(1)}, f32[3,17,17,129]{3,2,1,0:T(8,128)}, u32[]{:S(2)}) copy-start(f32[3,17,17,129]{3,2,1,0:T(8,128)} %get-tuple-element.21) | copy-start | bytes 1342120
  498.2 46.0 %copy-start.8 = (f32[3,17,17,129]{3,2,1,0:T(8,128)S(1)}, f32[3,17,17,129]{3,2,1,0:T(8,128)}, u32[]{:S(2)}) copy-start(f32[3,17,17,129]{3,2,1,0:T(8,128)} %get-tuple-element.17) | copy-start | bytes 1342120
  577.2 16.1 %collective-permute-start.29 = (f32[4,256,2]{2,1,0:T(8,128)S(1)}, f32[4,256,2]{2,1,0:T(8,128)S(1)}, u32[]{:S(2)}, u32[]{:S(2)}) collective-permute-start(f32[4,256,2]{2,1,0:T(8,128)S(1)} %get-tuple-element.91), channel_id=1, source_target_pairs={{64,0},{65,1},{66,2},{67,3},{68,4},{69,5},{70,6},{71,7},{72,8},{73... | collective-permute-start | bytes 24584 | tf_op jit(solution)/shard_map/ppermute | solution.py:26
  578.5 15.7 %collective-permute-start.28 = (f32[4,256,2]{2,1,0:T(8,128)S(1)}, f32[4,256,2]{2,1,0:T(8,128)S(1)}, u32[]{:S(2)}, u32[]{:S(2)}) collective-permute-start(f32[4,256,2]{2,1,0:T(8,128)S(1)} %get-tuple-element.90), channel_id=1, source_target_pairs={{0,64},{1,65},{2,66},{3,67},{4,68},{5,69},{6,70},{7,71},{8,72},{9,... | collective-permute-start | bytes 24584 | tf_op jit(solution)/shard_map/ppermute | solution.py:23
  594.8 14.4 %collective-permute-start.31 = (f32[2,256,132]{2,1,0:T(8,128)S(1)}, f32[2,256,132]{2,1,0:T(8,128)S(1)}, u32[]{:S(2)}, u32[]{:S(2)}) collective-permute-start(f32[2,256,132]{2,1,0:T(8,128)S(1)} %get-tuple-element.87), channel_id=1, source_target_pairs={{1,0},{2,1},{3,2},{4,3},{5,4},{6,5},{7,6},{8,7},{9,8},{10,9},{11,1... | collective-permute-start | bytes 811016 | tf_op jit(solution)/shard_map/ppermute | solution.py:26
  598.9 11.5 %collective-permute-start.30 = (f32[2,256,132]{2,1,0:T(8,128)S(1)}, f32[2,256,132]{2,1,0:T(8,128)S(1)}, u32[]{:S(2)}, u32[]{:S(2)}) collective-permute-start(f32[2,256,132]{2,1,0:T(8,128)S(1)} %get-tuple-element.86), channel_id=1, source_target_pairs={{0,1},{1,2},{2,3},{3,4},{4,5},{5,6},{6,7},{7,8},{8,9},{9,10},{10,1... | collective-permute-start | bytes 811016 | tf_op jit(solution)/shard_map/ppermute | solution.py:23
  (11 other events, 35.4 us)
